TPU v7x, 512 devices: a whole 4x4x16 slice. The times are simulated.
512 devices in a mesh: sect: 2 (over y_hi), exp: 32 (over z, y_lo), dp: 8 (over x, core).
Axes of the slice: x: 4, y: 4 (y_hi: 2, y_lo: 2; y = y_hi * 2 + y_lo), z: 16, core: 2. Of those that a mesh axis runs over, the one named last changes fastest.
Arguments:
- decode_states: bfloat16 [1024, 2048], P('exp'), may hold values from -15 to 15
- norm_gain: float32 [2048], replicated, may hold values from 0.25 to 1.75
- decode_routes: int32 [4, 1024, 2], P(None, 'exp'), may hold values from 0 to 31, all different within a row; in each aligned block of 32 rows (0 to 31, 32 to 63, ..., all dimensions but the last counted through in order) at most 3 rows name the same one
- decode_gates: float32 [4, 1024, 2], P(None, 'exp'), may hold values from 0.2 to 1
- up_weight: bfloat16 [2, 32, 1536, 2048], P('sect', 'exp', 'dp'), may hold values from -5 to 5
- down_weight: bfloat16 [2, 32, 1536, 2048], P('sect', 'exp', 'dp'), may hold values from -5 to 5
- traj_inputs: bfloat16 [2, 1024, 2048], P('sect', 'exp'), may hold values from -6 to 6
- traj_cotangents: bfloat16 [2, 1024, 2048], P('sect', 'exp'), may hold values from -6 to 6
- traj_lengths: int32 [32, 2, 16], P('exp'), may hold values from 1 to 4, 32 in all within a row
- packing: int32 [32, 32], P('exp'), may hold values from 0 to 31, each once within a row
- learner_routes: int32 [4096, 2], P('exp'), may hold values from 0 to 31, all different within a row; in each aligned block of 128 rows (0 to 127, 128 to 255, ...) at most 12 rows name the same one
- learner_gates: float32 [4096, 2], P('exp'), may hold values from 0.2 to 1
Outputs:
- final_states: bfloat16 [1024, 2048], P('exp', 'sect')
- fresh_up: bfloat16 [2, 32, 1536, 2048], P('sect', 'exp', 'dp')
- fresh_down: bfloat16 [2, 32, 1536, 2048], P('sect', 'exp', 'dp')
Inputs may be any that keep to these rules, and one draw needn't show every extreme that they name: `decode_routes`: within each aligned block of 32 rows of one step (the rows of one index of exp), no expert is named more than 3 times, and that bound is met. `learner_routes`: within each aligned block of 128 rows (the slots of one learner shard), no expert is named more than 12 times, and that bound is met. `traj_lengths`: each row of 16 lengths sums to 32 and its largest is 4. `packing`: each row is a permutation of the 32 learner shards, so every holder sends exactly one trajectory to every shard.
All inputs are finite; a program needn't handle non-finite values.
Results may differ from a plain program's by a relative error of at most 0.02.
Values may be sent and summed in bfloat16 or wider, within the bound.
A program may use at most 64 MiB of HBM per device.

v0:
```python
import jax
import jax.numpy as jnp
from jax import lax
from jax.sharding import PartitionSpec as P

step_size = 3.0
norm_eps = 1e-06


def partner(array, axis, apart):
    return lax.ppermute(array, axis, [(i, i ^ 1 << apart) for i in range(lax.axis_size(axis))])


def slot_table(routes, experts, capacity):
    flat_routes = routes.reshape(-1)
    member = (flat_routes[:, None] == jnp.arange(experts, dtype=jnp.int32)[None, :]).astype(
        jnp.int32
    )
    earlier = jnp.cumsum(member, axis=0) - member
    within = jnp.sum(earlier * member, axis=1)
    target = flat_routes * capacity + within
    one_hot = (target[:, None] == jnp.arange(experts * capacity, dtype=jnp.int32)[None, :]).astype(
        jnp.float32
    )
    return one_hot.reshape(routes.shape[0], routes.shape[1], experts * capacity)


def pack_trajectories(held_rows, lengths, row_pack, capacity):
    traj_count = lengths.shape[1]
    per_half = held_rows.shape[0] // 2
    column_ids = jnp.arange(row_pack.shape[0], dtype=jnp.int32)
    starts = jnp.cumsum(lengths, axis=1) - lengths
    matches = (row_pack[None, :] == column_ids[:, None]).astype(jnp.int32)
    chosen = jnp.sum(matches * column_ids[None, :], axis=1)
    half_index = chosen // traj_count
    length_of = jnp.take(lengths.reshape(-1), chosen)
    first_row = half_index * per_half + jnp.take(starts.reshape(-1), chosen)
    offsets = jnp.arange(capacity, dtype=jnp.int32)
    in_length = offsets[None, :] < length_of[:, None]
    row_index = jnp.where(in_length, first_row[:, None] + offsets[None, :], 0).reshape(-1)
    picked = jnp.take(held_rows, row_index, axis=0)
    return jnp.where(in_length.reshape(-1)[:, None, None], picked, jnp.zeros_like(picked))


def across(block):
    return partner(block, "sect", 0)


def to_experts(payload):
    arrived = lax.all_to_all(payload, "exp", split_axis=0, concat_axis=0, tiled=True)
    return arrived


def sum_and_return(partial_out):
    summed = lax.psum(partial_out.astype(jnp.bfloat16), "dp")
    returned = lax.all_to_all(summed, "exp", split_axis=0, concat_axis=0, tiled=True)
    return returned


def expert_forward(arrived, up_slice, down_slice, hidden_total):
    inputs = arrived[:, 0, :]
    before_act = jnp.einsum(
        "sd,hd->sh", inputs, up_slice, preferred_element_type=jnp.float32
    ) * inputs.shape[1] ** (-0.5)
    activated = jax.nn.silu(before_act).astype(jnp.bfloat16)
    return jnp.einsum(
        "sh,hd->sd", activated, down_slice, preferred_element_type=jnp.float32
    ) * hidden_total ** (-0.5)


def learner_update(arrived, up_slice, down_slice, hidden_total):
    inputs = arrived[:, 0, :]
    scaled_grad = arrived[:, 1, :]
    model_scale = inputs.shape[1] ** (-0.5)
    hidden_scale = hidden_total ** (-0.5)
    before_act = (
        jnp.einsum("sd,hd->sh", inputs, up_slice, preferred_element_type=jnp.float32) * model_scale
    )
    sigmoid_val = jax.nn.sigmoid(before_act)
    activated = (before_act * sigmoid_val).astype(jnp.bfloat16)
    hidden_grad = (
        jnp.einsum("sd,hd->sh", scaled_grad, down_slice, preferred_element_type=jnp.float32)
        * hidden_scale
    )
    pre_grad = (hidden_grad * sigmoid_val * (1.0 + before_act * (1.0 - sigmoid_val))).astype(
        jnp.bfloat16
    )
    down_grad = (
        jnp.einsum("sh,sd->hd", activated, scaled_grad, preferred_element_type=jnp.float32)
        * hidden_scale
    )
    up_grad = (
        jnp.einsum("sh,sd->hd", pre_grad, inputs, preferred_element_type=jnp.float32) * model_scale
    )
    new_up = (up_slice.astype(jnp.float32) - step_size * up_grad).astype(jnp.bfloat16)
    new_down = (down_slice.astype(jnp.float32) - step_size * down_grad).astype(jnp.bfloat16)
    return jnp.stack([new_up, new_down])


def decode_step(
    states, norm_gain, routes, gate_values, up_slice, down_slice, is_rollout, hidden_total
):
    experts = lax.axis_size("exp")
    capacity = 3 * routes.shape[0] * routes.shape[1] // (2 * experts)
    normed = (
        states * lax.rsqrt(jnp.mean(states * states, axis=1, keepdims=True) + norm_eps) * norm_gain
    )
    normed = normed.astype(jnp.bfloat16)
    one_hot = slot_table(routes, experts, capacity)
    outgoing = jnp.einsum(
        "rks,rd->sd", one_hot.astype(jnp.bfloat16), normed, preferred_element_type=jnp.float32
    )
    arrived = to_experts(outgoing.astype(jnp.bfloat16)[:, None, :])
    partial_out = lax.cond(
        is_rollout,
        lambda: expert_forward(arrived, up_slice, down_slice, hidden_total),
        lambda: jnp.zeros((arrived.shape[0], arrived.shape[2]), jnp.float32),
    )
    returned = sum_and_return(partial_out)
    weighted = one_hot * gate_values[:, :, None]
    mixed = jnp.einsum(
        "rks,sd->rd", weighted, returned.astype(jnp.float32), precision=lax.Precision.HIGHEST
    )
    return states + mixed


def on_device(
    decode_states,
    norm_gain,
    decode_routes,
    decode_gates,
    up_weight,
    down_weight,
    traj_inputs,
    traj_cotangents,
    traj_lengths,
    packing,
    learner_routes,
    learner_gates,
):
    experts = lax.axis_size("exp")
    is_learner = lax.axis_index("sect") == 1
    is_rollout = jnp.logical_not(is_learner)
    up_here = up_weight[0, 0]
    down_here = down_weight[0, 0]
    hidden_total = up_here.shape[0] * lax.axis_size("dp")
    held_pair = jnp.stack([traj_inputs[0], traj_cotangents[0]], axis=1)
    crossed = across(held_pair)
    held_rows = jnp.concatenate([crossed, held_pair], axis=0)

    def run_steps(states, first_step, last_step, up_mat, down_mat):
        for step_index in range(first_step, last_step):
            states = decode_step(
                states,
                norm_gain,
                decode_routes[step_index],
                decode_gates[step_index],
                up_mat,
                down_mat,
                is_rollout,
                hidden_total,
            )
        return states

    total_steps = decode_routes.shape[0]
    half_steps = total_steps // 2
    states = decode_states.astype(jnp.float32)
    capacity_t = learner_routes.shape[0] // experts
    outgoing = pack_trajectories(held_rows, traj_lengths[0], packing[0], capacity_t)
    packed = lax.all_to_all(outgoing, "exp", split_axis=0, concat_axis=0, tiled=True)
    capacity_l = 3 * learner_routes.shape[0] * learner_routes.shape[1] // (2 * experts)
    one_hot = slot_table(learner_routes, experts, capacity_l).astype(jnp.bfloat16)
    token_part = jnp.einsum(
        "rks,rd->sd", one_hot, packed[:, 0, :], preferred_element_type=jnp.float32
    )
    scaled_rows = (learner_gates[:, :, None] * packed[:, 1, None, :].astype(jnp.float32)).astype(
        jnp.bfloat16
    )
    grad_part = jnp.einsum("rks,rkd->sd", one_hot, scaled_rows, preferred_element_type=jnp.float32)
    payload = jnp.stack([token_part, grad_part], axis=1).astype(jnp.bfloat16)
    arrived = to_experts(payload)
    fresh_pair = lax.cond(
        is_learner,
        lambda: learner_update(arrived, up_here, down_here, hidden_total),
        lambda: jnp.zeros((2,) + up_here.shape, jnp.bfloat16),
    )
    returned = across(fresh_pair)
    fresh_here = jnp.where(is_learner, fresh_pair, returned)
    states = run_steps(states, 0, half_steps, up_here, down_here)
    states = run_steps(states, half_steps, total_steps, fresh_here[0], fresh_here[1])
    half_width = states.shape[1] // 2
    own_half = states[:, :half_width].astype(jnp.bfloat16)
    other_half = states[:, half_width:].astype(jnp.bfloat16)
    delivered = across(other_half)
    final_states = jnp.where(is_learner, delivered, own_half)
    return (final_states, fresh_here[0][None, None], fresh_here[1][None, None])


def solution(mesh):
    in_specs = (
        P("exp", None),
        P(),
        P(None, "exp", None),
        P(None, "exp", None),
        P("sect", "exp", "dp", None),
        P("sect", "exp", "dp", None),
        P("sect", "exp", None),
        P("sect", "exp", None),
        P("exp", None, None),
        P("exp", None),
        P("exp", None),
        P("exp", None),
    )
    out_specs = (P("exp", "sect"), P("sect", "exp", "dp", None), P("sect", "exp", "dp", None))
    return jax.shard_map(
        on_device, mesh=mesh, in_specs=in_specs, out_specs=out_specs, check_vma=False
    )
```

profile of v0, /device:TPU:14, one launch (start us, length us, event | category | flops | bytes accessed | tf_op | source)
XLA Modules:
  0.0 829.9 jit_solution(11071036561187698457)
XLA Ops:
  17.2 16.7 %all-to-all-start = ((bf16[32,2,3072]{2,1,0:T(2,128)(2,1)}), bf16[32,2,3072]{2,1,0:T(2,128)(2,1)S(1)}, u32[]{:S(2)}, u32[]{:S(2)}) async-start(bf16[32,2,3072]{2,1,0:T(2,128)(2,1)} %reshape.297), calls=%async_computation | async-start | bytes 786432 | tf_op jit(solution)/shard_map/all_to_all | solution.py:50
  34.0 27.1 %all-to-all-done = bf16[32,2,3072]{2,1,0:T(2,128)(2,1)S(1)} async-done(((bf16[32,2,3072]{2,1,0:T(2,128)(2,1)}), bf16[32,2,3072]{2,1,0:T(2,128)(2,1)S(1)}, u32[]{:S(2)}, u32[]{:S(2)}) %all-to-all-start) | async-done | bytes 393248 | tf_op jit(solution)/shard_map/all_to_all | solution.py:50
  63.3 65.0 %all-reduce.5.cloned.1.call-done = bf16[32,3,2048]{2,1,0:T(4,128)(2,1)} async-done(((bf16[32,3,2048]{2,1,0:T(4,128)(2,1)}), bf16[32,3,2048]{2,1,0:T(4,128)(2,1)}) %all-reduce.5.cloned.1.call-update) | async-done | bytes 393232 | tf_op jit(solution)/shard_map/psum | solution.py:55
  128.3 13.8 %all-to-all-start.1 = ((bf16[32,3,2048]{2,1,0:T(4,128)(2,1)}), bf16[32,3,2048]{2,1,0:T(4,128)(2,1)S(1)}, u32[]{:S(2)}, u32[]{:S(2)}) async-start(bf16[32,3,2048]{2,1,0:T(4,128)(2,1)} %all-reduce.5.cloned.1.call-done), calls=%async_computation.1 | async-start | bytes 1048576 | tf_op jit(solution)/shard_map/all_to_all | solution.py:56
  143.2 4.0 collective-permute-start
  149.4 26.4 %all-to-all-done.1 = bf16[32,3,2048]{2,1,0:T(4,128)(2,1)S(1)} async-done(((bf16[32,3,2048]{2,1,0:T(4,128)(2,1)}), bf16[32,3,2048]{2,1,0:T(4,128)(2,1)S(1)}, u32[]{:S(2)}, u32[]{:S(2)}) %all-to-all-start.1) | async-done | bytes 393248 | tf_op jit(solution)/shard_map/all_to_all | solution.py:56
  179.5 4.0 all-to-all-start.2
  184.6 2.7 gather_fusion
  187.3 2.6 broadcast_select_fusion.1
  189.8 21.4 %all-to-all-done.2 = bf16[32,2,3072]{2,1,0:T(2,128)(2,1)S(1)} async-done(((bf16[32,2,3072]{2,1,0:T(2,128)(2,1)}), bf16[32,2,3072]{2,1,0:T(2,128)(2,1)S(1)}, u32[]{:S(2)}, u32[]{:S(2)}) %all-to-all-start.2) | async-done | bytes 393248 | tf_op jit(solution)/shard_map/all_to_all | solution.py:50
  211.2 4.3 all-to-all-start.5
  220.4 48.1 %all-to-all-done.5 = bf16[128,2,2048]{2,1,0:T(2,128)(2,1)S(1)} async-done(((bf16[128,2,2048]{2,1,0:T(2,128)(2,1)}), bf16[128,2,2048]{2,1,0:T(2,128)(2,1)S(1)}, u32[]{:S(2)}, u32[]{:S(2)}) %all-to-all-start.5) | async-done | bytes 1048608 | tf_op jit(solution)/shard_map/all_to_all | solution.py:170
  268.5 25.5 %all-reduce.7.cloned.1.call-done = bf16[32,3,2048]{2,1,0:T(4,128)(2,1)} async-done(((bf16[32,3,2048]{2,1,0:T(4,128)(2,1)}), bf16[32,3,2048]{2,1,0:T(4,128)(2,1)}) %all-reduce.7.cloned.1.call-update) | async-done | bytes 393232 | tf_op jit(solution)/shard_map/psum | solution.py:55
  294.0 13.8 %all-to-all-start.3 = ((bf16[32,3,2048]{2,1,0:T(4,128)(2,1)}), bf16[32,3,2048]{2,1,0:T(4,128)(2,1)S(1)}, u32[]{:S(2)}, u32[]{:S(2)}) async-start(bf16[32,3,2048]{2,1,0:T(4,128)(2,1)} %all-reduce.7.cloned.1.call-done), calls=%async_computation.3 | async-start | bytes 1048576 | tf_op jit(solution)/shard_map/all_to_all | solution.py:56
  311.7 4.9 copy.159
  316.6 24.9 %all-to-all-done.3 = bf16[32,3,2048]{2,1,0:T(4,128)(2,1)S(1)} async-done(((bf16[32,3,2048]{2,1,0:T(4,128)(2,1)}), bf16[32,3,2048]{2,1,0:T(4,128)(2,1)S(1)}, u32[]{:S(2)}, u32[]{:S(2)}) %all-to-all-start.3) | async-done | bytes 393248 | tf_op jit(solution)/shard_map/all_to_all | solution.py:56
  342.3 4.1 all-to-all-start.6
  350.0 142.2 %all-to-all-done.6 = bf16[384,2,2048]{2,1,0:T(2,128)(2,1)S(1)} async-done(((bf16[384,2,2048]{2,1,0:T(2,128)(2,1)}), bf16[384,2,2048]{2,1,0:T(2,128)(2,1)S(1)}, u32[]{:S(2)}, u32[]{:S(2)}) %all-to-all-start.6) | async-done | bytes 3145760 | tf_op jit(solution)/shard_map/all_to_all | solution.py:50
  492.6 13.6 %collective-permute-start.1 = (bf16[2,192,2048]{2,1,0:T(8,128)(2,1)S(1)}, bf16[2,192,2048]{2,1,0:T(8,128)(2,1)S(1)}, u32[]{:S(2)}, u32[]{:S(2)}) collective-permute-start(bf16[2,192,2048]{2,1,0:T(8,128)(2,1)S(1)} %get-tuple-element.162), channel_id=1, source_target_pairs={{0,256},{256,0},{1,257},{257,1},{2,258},{258,2},{3,259},{259,3},{4... | collective-permute-start | bytes 4718600 | tf_op jit(solution)/shard_map/ppermute | solution.py:11
  507.3 2.5 reduce.4
  511.8 4.4 all-to-all-start.4
  516.3 25.9 %all-to-all-done.4 = bf16[32,2,3072]{2,1,0:T(2,128)(2,1)} async-done(((bf16[32,2,3072]{2,1,0:T(2,128)(2,1)}), bf16[32,2,3072]{2,1,0:T(2,128)(2,1)}, u32[]{:S(2)}, u32[]{:S(2)}) %all-to-all-start.4) | async-done | bytes 393248 | tf_op jit(solution)/shard_map/all_to_all | solution.py:50
  542.1 3.4 reshape.302
  550.3 66.9 %all-reduce.9.cloned.1.call-done = bf16[32,3,2048]{2,1,0:T(4,128)(2,1)} async-done(((bf16[32,3,2048]{2,1,0:T(4,128)(2,1)}), bf16[32,3,2048]{2,1,0:T(4,128)(2,1)}) %all-reduce.9.cloned.1.call-update) | async-done | bytes 393232 | tf_op jit(solution)/shard_map/psum | solution.py:55
  617.2 13.8 %all-to-all-start.7 = ((bf16[32,3,2048]{2,1,0:T(4,128)(2,1)}), bf16[32,3,2048]{2,1,0:T(4,128)(2,1)S(1)}, u32[]{:S(2)}, u32[]{:S(2)}) async-start(bf16[32,3,2048]{2,1,0:T(4,128)(2,1)} %all-reduce.9.cloned.1.call-done), calls=%async_computation.7 | async-start | bytes 1048576 | tf_op jit(solution)/shard_map/all_to_all | solution.py:56
  631.1 33.6 %all-to-all-done.7 = bf16[32,3,2048]{2,1,0:T(4,128)(2,1)S(1)} async-done(((bf16[32,3,2048]{2,1,0:T(4,128)(2,1)}), bf16[32,3,2048]{2,1,0:T(4,128)(2,1)S(1)}, u32[]{:S(2)}, u32[]{:S(2)}) %all-to-all-start.7) | async-done | bytes 393248 | tf_op jit(solution)/shard_map/all_to_all | solution.py:56
  667.7 4.0 all-to-all-start.8
  671.7 27.7 %all-to-all-done.8 = bf16[32,2,3072]{2,1,0:T(2,128)(2,1)S(1)} async-done(((bf16[32,2,3072]{2,1,0:T(2,128)(2,1)}), bf16[32,2,3072]{2,1,0:T(2,128)(2,1)S(1)}, u32[]{:S(2)}, u32[]{:S(2)}) %all-to-all-start.8) | async-done | bytes 393248 | tf_op jit(solution)/shard_map/all_to_all | solution.py:50
  703.4 63.5 %all-reduce.11.cloned.1.call-done = bf16[32,3,2048]{2,1,0:T(4,128)(2,1)} async-done(((bf16[32,3,2048]{2,1,0:T(4,128)(2,1)}), bf16[32,3,2048]{2,1,0:T(4,128)(2,1)}) %all-reduce.11.cloned.1.call-update) | async-done | bytes 393232 | tf_op jit(solution)/shard_map/psum | solution.py:55
  767.0 47.5 %all_to_all.78 = bf16[32,3,2048]{2,1,0:T(4,128)(2,1)S(1)} all-to-all(bf16[32,3,2048]{2,1,0:T(4,128)(2,1)} %all-reduce.11.cloned.1.call-done), channel_id=1, replica_groups=mesh['sect'=2,'exp'=32,'dp'=8] {'exp'}, dimensions={0} | all-to-all | bytes 786432 | tf_op jit(solution)/shard_map/all_to_all | solution.py:56
  815.1 4.0 collective-permute-start.2
  819.1 3.6 collective-permute-done.2
  (155 shorter events, 56.6 us)
Async XLA Ops:
  16.2 45.2 %copy-start.12 = (bf16[1,1,192,2048]{3,2,1,0:T(8,128)(2,1)S(1)}, bf16[1,1,192,2048]{3,2,1,0:T(8,128)(2,1)}, u32[]{:S(2)}) copy-start(bf16[1,1,192,2048]{3,2,1,0:T(8,128)(2,1)} %param.28) | copy-start | bytes 2359300
  16.2 45.2 %copy-start.14 = (bf16[1,1,192,2048]{3,2,1,0:T(8,128)(2,1)S(1)}, bf16[1,1,192,2048]{3,2,1,0:T(8,128)(2,1)}, u32[]{:S(2)}) copy-start(bf16[1,1,192,2048]{3,2,1,0:T(8,128)(2,1)} %param.29) | copy-start | bytes 2359300
  17.2 43.8 %all-to-all-start = ((bf16[32,2,3072]{2,1,0:T(2,128)(2,1)}), bf16[32,2,3072]{2,1,0:T(2,128)(2,1)S(1)}, u32[]{:S(2)}, u32[]{:S(2)}) async-start(bf16[32,2,3072]{2,1,0:T(2,128)(2,1)} %reshape.297), calls=%async_computation | async-start | bytes 786432 | tf_op jit(solution)/shard_map/all_to_all | solution.py:50
  33.9 94.4 %all-reduce.5.cloned.1.call-start = ((), (), s32[]{:S(2)}) async-start(), calls=%async_computation.10 | async-start | bytes 1048576 | tf_op jit(solution)/shard_map/psum | solution.py:55
  62.2 79.9 %copy-start.7 = (bf16[1,32,2048]{2,1,0:T(8,128)(2,1)S(1)}, bf16[1,32,2048]{2,1,0:T(8,128)(2,1)}, u32[]{:S(2)}) copy-start(bf16[1,32,2048]{2,1,0:T(8,128)(2,1)} %param.30) | copy-start | bytes 393220
  62.2 80.1 %copy-start.8 = (bf16[1,32,2048]{2,1,0:T(8,128)(2,1)S(1)}, bf16[1,32,2048]{2,1,0:T(8,128)(2,1)}, u32[]{:S(2)}) copy-start(bf16[1,32,2048]{2,1,0:T(8,128)(2,1)} %param.31) | copy-start | bytes 393220
  63.3 83.9 %copy-start.11 = (s32[1,2,16]{2,1,0:T(2,128)S(1)}, s32[1,2,16]{2,1,0:T(2,128)}, u32[]{:S(2)}) copy-start(s32[1,2,16]{2,1,0:T(2,128)} %param.32) | copy-start | bytes 388
  63.3 84.3 %copy-start.15 = (s32[1,32]{1,0:T(1,128)S(1)}, s32[1,32]{1,0:T(1,128)}, u32[]{:S(2)}) copy-start(s32[1,32]{1,0:T(1,128)} %param.33) | copy-start | bytes 388
  128.3 47.5 %all-to-all-start.1 = ((bf16[32,3,2048]{2,1,0:T(4,128)(2,1)}), bf16[32,3,2048]{2,1,0:T(4,128)(2,1)S(1)}, u32[]{:S(2)}, u32[]{:S(2)}) async-start(bf16[32,3,2048]{2,1,0:T(4,128)(2,1)} %all-reduce.5.cloned.1.call-done), calls=%async_computation.1 | async-start | bytes 1048576 | tf_op jit(solution)/shard_map/all_to_all | solution.py:56
  142.3 33.8 %copy-start.4 = (bf16[32,2048]{1,0:T(8,128)(2,1)S(1)}, bf16[32,2048]{1,0:T(8,128)(2,1)}, u32[]{:S(2)}) copy-start(bf16[32,2048]{1,0:T(8,128)(2,1)} %param.24) | copy-start | bytes 393220
  143.2 34.1 %copy-start.6 = (f32[2048]{0:T(1024)S(1)}, f32[2048]{0:T(1024)}, u32[]{:S(2)}) copy-start(f32[2048]{0:T(1024)} %param.25) | copy-start | bytes 24580
  143.2 40.6 %collective-permute-start = (bf16[32,2,2048]{2,1,0:T(2,128)(2,1)S(1)}, bf16[32,2,2048]{2,1,0:T(2,128)(2,1)S(1)}, u32[]{:S(2)}, u32[]{:S(2)}) collective-permute-start(bf16[32,2,2048]{2,1,0:T(2,128)(2,1)S(1)} %pad_maximum_fusion.2), channel_id=1, source_target_pairs={{0,256},{256,0},{1,257},{257,1},{2,258},{258,2},{3,259},{259,3},{4... | collective-permute-start | bytes 786440 | tf_op jit(solution)/shard_map/ppermute | solution.py:11
  176.5 0.7 copy-start.2
  179.5 31.7 %all-to-all-start.2 = ((bf16[32,2,3072]{2,1,0:T(2,128)(2,1)}), bf16[32,2,3072]{2,1,0:T(2,128)(2,1)S(1)}, u32[]{:S(2)}, u32[]{:S(2)}) async-start(bf16[32,2,3072]{2,1,0:T(2,128)(2,1)} %reshape.299), calls=%async_computation.2 | async-start | bytes 786432 | tf_op jit(solution)/shard_map/all_to_all | solution.py:50
  189.8 25.7 %copy-start.9 = (s32[128,2]{0,1:T(2,128)S(1)}, s32[128,2]{0,1:T(2,128)}, u32[]{:S(2)}) copy-start(s32[128,2]{0,1:T(2,128)} %param.34) | copy-start | bytes 3076
  211.2 57.3 %all-to-all-start.5 = ((bf16[128,2,2048]{2,1,0:T(2,128)(2,1)}), bf16[128,2,2048]{2,1,0:T(2,128)(2,1)S(1)}, u32[]{:S(2)}, u32[]{:S(2)}) async-start(bf16[128,2,2048]{2,1,0:T(2,128)(2,1)} %broadcast_select_fusion.1), calls=%async_computation.5 | async-start | bytes 2097152 | tf_op jit(solution)/shard_map/all_to_all | solution.py:170
  215.5 78.5 %all-reduce.7.cloned.1.call-start = ((), (), s32[]{:S(2)}) async-start(), calls=%async_computation.11 | async-start | bytes 1048576 | tf_op jit(solution)/shard_map/psum | solution.py:55
  294.0 47.5 %all-to-all-start.3 = ((bf16[32,3,2048]{2,1,0:T(4,128)(2,1)}), bf16[32,3,2048]{2,1,0:T(4,128)(2,1)S(1)}, u32[]{:S(2)}, u32[]{:S(2)}) async-start(bf16[32,3,2048]{2,1,0:T(4,128)(2,1)} %all-reduce.7.cloned.1.call-done), calls=%async_computation.3 | async-start | bytes 1048576 | tf_op jit(solution)/shard_map/all_to_all | solution.py:56
  310.0 0.7 copy-start.10
  341.5 0.8 copy-start.3
  342.3 149.9 %all-to-all-start.6 = ((bf16[384,2,2048]{2,1,0:T(2,128)(2,1)}), bf16[384,2,2048]{2,1,0:T(2,128)(2,1)S(1)}, u32[]{:S(2)}, u32[]{:S(2)}) async-start(bf16[384,2,2048]{2,1,0:T(2,128)(2,1)} %copy.159), calls=%async_computation.6 | async-start | bytes 6291456 | tf_op jit(solution)/shard_map/all_to_all | solution.py:50
  492.6 53.0 %collective-permute-start.1 = (bf16[2,192,2048]{2,1,0:T(8,128)(2,1)S(1)}, bf16[2,192,2048]{2,1,0:T(8,128)(2,1)S(1)}, u32[]{:S(2)}, u32[]{:S(2)}) collective-permute-start(bf16[2,192,2048]{2,1,0:T(8,128)(2,1)S(1)} %get-tuple-element.162), channel_id=1, source_target_pairs={{0,256},{256,0},{1,257},{257,1},{2,258},{258,2},{3,259},{259,3},{4... | collective-permute-start | bytes 4718600 | tf_op jit(solution)/shard_map/ppermute | solution.py:11
  511.8 30.3 %all-to-all-start.4 = ((bf16[32,2,3072]{2,1,0:T(2,128)(2,1)}), bf16[32,2,3072]{2,1,0:T(2,128)(2,1)}, u32[]{:S(2)}, u32[]{:S(2)}) async-start(bf16[32,2,3072]{2,1,0:T(2,128)(2,1)} %reshape.301), calls=%async_computation.4 | async-start | bytes 786432 | tf_op jit(solution)/shard_map/all_to_all | solution.py:50
  516.2 101.0 %all-reduce.9.cloned.1.call-start = ((), (), s32[]{:S(2)}) async-start(), calls=%async_computation.12 | async-start | bytes 1048576 | tf_op jit(solution)/shard_map/psum | solution.py:55
  617.2 47.5 %all-to-all-start.7 = ((bf16[32,3,2048]{2,1,0:T(4,128)(2,1)}), bf16[32,3,2048]{2,1,0:T(4,128)(2,1)S(1)}, u32[]{:S(2)}, u32[]{:S(2)}) async-start(bf16[32,3,2048]{2,1,0:T(4,128)(2,1)} %all-reduce.9.cloned.1.call-done), calls=%async_computation.7 | async-start | bytes 1048576 | tf_op jit(solution)/shard_map/all_to_all | solution.py:56
  667.7 31.7 %all-to-all-start.8 = ((bf16[32,2,3072]{2,1,0:T(2,128)(2,1)}), bf16[32,2,3072]{2,1,0:T(2,128)(2,1)S(1)}, u32[]{:S(2)}, u32[]{:S(2)}) async-start(bf16[32,2,3072]{2,1,0:T(2,128)(2,1)} %reshape.303), calls=%async_computation.8 | async-start | bytes 786432 | tf_op jit(solution)/shard_map/all_to_all | solution.py:50
  671.7 95.3 %all-reduce.11.cloned.1.call-start = ((), (), s32[]{:S(2)}) async-start(), calls=%async_computation.13 | async-start | bytes 1048576 | tf_op jit(solution)/shard_map/psum | solution.py:55
  815.1 7.7 collective-permute-start.2
Sparse Core Ops, SparseCore 0:
  63.4 64.8 all-reduce.4
  219.5 74.4 all-reduce.6
  550.4 66.7 all-reduce.8
  703.6 63.3 all-reduce.10
where the time goes:
time: 831 us; the launch traced here: 830 us
  waiting for transfers between devices  602 us (72%)
  starting transfers between devices  101 us (12%)
  blocking collectives  47.5 us (6%)
  local copies, waits for them, and re-layouts  35.2 us (4%)
  other arithmetic  16.6 us (2%)
  between operations  14.4 us (2%)
  matrix products  13.5 us (2%)
    all_to_all x5, waiting for transfers between devices, to_experts(): lax.all_to_all(payload, 'exp', split_axis=0, concat_axis=0, tiled=True)  244 us
    psum x4, waiting for transfers between devices, sum_and_return(): summed = lax.psum(partial_out.astype(jnp.bfloat16), 'dp')  221 us
    all_to_all x3, waiting for transfers between devices, sum_and_return(): lax.all_to_all(summed, 'exp', split_axis=0, concat_axis=0, tiled=True)  84.9 us
    all_to_all x1, waiting for transfers between devices, on_device(): lax.all_to_all(outgoing, 'exp', split_axis=0, concat_axis=0, tiled=True)  48.1 us
    all_to_all x1, blocking collectives, sum_and_return(): lax.all_to_all(summed, 'exp', split_axis=0, concat_axis=0, tiled=True)  47.5 us
    all_to_all x3, starting transfers between devices, sum_and_return(): lax.all_to_all(summed, 'exp', split_axis=0, concat_axis=0, tiled=True)  41.4 us
    all_to_all x5, starting transfers between devices, to_experts(): lax.all_to_all(payload, 'exp', split_axis=0, concat_axis=0, tiled=True)  33.2 us
    ppermute x3, starting transfers between devices, partner(): lax.ppermute(array, axis, [(i, i ^ 1 << apart) for i in range(lax.axis_si...  21.6 us
  transfers between devices with their start and end apart: 16, of which 14 were waited for; matrix products, arithmetic and copies ran while one was open for 4% of the time, Pallas kernels for 0%

commit v1 on v0

--- a/solution.py
+++ b/solution.py
@@ -52,7 +52,7 @@
 
 
 def sum_and_return(partial_out):
-    summed = lax.psum(partial_out.astype(jnp.bfloat16), "dp")
+    summed = jnp.sum(lax.all_gather(partial_out.astype(jnp.bfloat16), "dp"), axis=0)
     returned = lax.all_to_all(summed, "exp", split_axis=0, concat_axis=0, tiled=True)
     return returned
 

time: 831 us -> 654 us (0.79)
  the two profiles are of different devices: /device:TPU:14 before, /device:TPU:16 now
where the time goes in v1:
time: 654 us; the launch traced here: 653 us
  waiting for transfers between devices  435 us (67%)
  starting transfers between devices  81.1 us (12%)
  blocking collectives  46.4 us (7%)
  local copies, waits for them, and re-layouts  36.6 us (6%)
  other arithmetic  25.6 us (4%)
  between operations  14.5 us (2%)
  matrix products  13.3 us (2%)
    all_to_all x5, waiting for transfers between devices, to_experts(): lax.all_to_all(payload, 'exp', split_axis=0, concat_axis=0, tiled=True)  177 us
    all_gather x4, waiting for transfers between devices, sum_and_return(): lax.all_gather(partial_out.astype(jnp.bfloat16), 'dp')  109 us
    all_to_all x3, waiting for transfers between devices, sum_and_return(): lax.all_to_all(summed, 'exp', split_axis=0, concat_axis=0, tiled=True)  81.2 us
    all_to_all x1, waiting for transfers between devices, on_device(): lax.all_to_all(outgoing, 'exp', split_axis=0, concat_axis=0, tiled=True)  49 us
    all_to_all x1, blocking collectives, sum_and_return(): lax.all_to_all(summed, 'exp', split_axis=0, concat_axis=0, tiled=True)  46.4 us
    all_to_all x3, starting transfers between devices, sum_and_return(): lax.all_to_all(summed, 'exp', split_axis=0, concat_axis=0, tiled=True)  34.8 us
    all_to_all x5, starting transfers between devices, to_experts(): lax.all_to_all(payload, 'exp', split_axis=0, concat_axis=0, tiled=True)  32.9 us
    ppermute x3, waiting for transfers between devices, partner(): lax.ppermute(array, axis, [(i, i ^ 1 << apart) for i in range(lax.axis_si...  19 us
  transfers between devices with their start and end apart: 16, of which 15 were waited for; matrix products, arithmetic and copies ran while one was open for 7% of the time, Pallas kernels for 0%

profile of v1, /device:TPU:16, one launch (start us, length us, event | category | flops | bytes accessed | tf_op | source)
XLA Modules:
  0.0 652.7 jit_solution(15290496039093183195)
XLA Ops:
  17.1 16.2 %all-to-all-start = ((bf16[32,2,3072]{2,1,0:T(2,128)(2,1)}), bf16[32,2,3072]{2,1,0:T(2,128)(2,1)S(1)}, u32[]{:S(2)}, u32[]{:S(2)}) async-start(bf16[32,2,3072]{2,1,0:T(2,128)(2,1)} %reshape.301), calls=%async_computation | async-start | bytes 786432 | tf_op jit(solution)/shard_map/all_to_all | solution.py:50
  33.4 27.4 %all-to-all-done = bf16[32,2,3072]{2,1,0:T(2,128)(2,1)S(1)} async-done(((bf16[32,2,3072]{2,1,0:T(2,128)(2,1)}), bf16[32,2,3072]{2,1,0:T(2,128)(2,1)S(1)}, u32[]{:S(2)}, u32[]{:S(2)}) %all-to-all-start) | async-done | bytes 393248 | tf_op jit(solution)/shard_map/all_to_all | solution.py:50
  63.1 4.5 collective-permute-start
  69.7 19.9 %all-gather.9.cloned.1.call-done = bf16[768,2048]{1,0:T(8,128)(2,1)} async-done(((bf16[96,2048]{1,0:T(8,128)(2,1)}), bf16[768,2048]{1,0:T(8,128)(2,1)}) %all-gather.9.cloned.1.call-update) | async-done | bytes 3145744 | tf_op jit(solution)/shard_map/all_gather | solution.py:55
  93.1 13.2 %all-to-all-start.1 = ((bf16[32,3,2048]{2,1,0:T(4,128)(2,1)}), bf16[32,3,2048]{2,1,0:T(4,128)(2,1)S(1)}, u32[]{:S(2)}, u32[]{:S(2)}) async-start(bf16[32,3,2048]{2,1,0:T(4,128)(2,1)} %all_to_all.51), calls=%async_computation.1 | async-start | bytes 1048576 | tf_op jit(solution)/shard_map/all_to_all | solution.py:56
  112.7 27.0 %all-to-all-done.1 = bf16[32,3,2048]{2,1,0:T(4,128)(2,1)S(1)} async-done(((bf16[32,3,2048]{2,1,0:T(4,128)(2,1)}), bf16[32,3,2048]{2,1,0:T(4,128)(2,1)S(1)}, u32[]{:S(2)}, u32[]{:S(2)}) %all-to-all-start.1) | async-done | bytes 393248 | tf_op jit(solution)/shard_map/all_to_all | solution.py:56
  139.7 4.1 all-to-all-start.5
  148.1 49.0 %all-to-all-done.5 = bf16[128,2,2048]{2,1,0:T(2,128)(2,1)S(1)} async-done(((bf16[128,2,2048]{2,1,0:T(2,128)(2,1)}), bf16[128,2,2048]{2,1,0:T(2,128)(2,1)S(1)}, u32[]{:S(2)}, u32[]{:S(2)}) %all-to-all-start.5) | async-done | bytes 1048608 | tf_op jit(solution)/shard_map/all_to_all | solution.py:170
  197.1 4.9 all-to-all-start.2
  205.8 4.9 copy.159
  210.7 18.5 %all-to-all-done.2 = bf16[32,2,3072]{2,1,0:T(2,128)(2,1)S(1)} async-done(((bf16[32,2,3072]{2,1,0:T(2,128)(2,1)}), bf16[32,2,3072]{2,1,0:T(2,128)(2,1)S(1)}, u32[]{:S(2)}, u32[]{:S(2)}) %all-to-all-start.2) | async-done | bytes 393248 | tf_op jit(solution)/shard_map/all_to_all | solution.py:50
  230.0 4.1 all-to-all-start.6
  234.1 3.5 reshape.304
  238.4 36.3 %all-gather.11.cloned.1.call-done = bf16[768,2048]{1,0:T(8,128)(2,1)} async-done(((bf16[96,2048]{1,0:T(8,128)(2,1)}), bf16[768,2048]{1,0:T(8,128)(2,1)}) %all-gather.11.cloned.1.call-update) | async-done | bytes 3145744 | tf_op jit(solution)/shard_map/all_gather | solution.py:55
  274.7 3.3 reduce_sum.240
  280.1 93.0 %all-to-all-done.6 = bf16[384,2,2048]{2,1,0:T(2,128)(2,1)S(1)} async-done(((bf16[384,2,2048]{2,1,0:T(2,128)(2,1)}), bf16[384,2,2048]{2,1,0:T(2,128)(2,1)S(1)}, u32[]{:S(2)}, u32[]{:S(2)}) %all-to-all-start.6) | async-done | bytes 3145760 | tf_op jit(solution)/shard_map/all_to_all | solution.py:50
  373.1 8.4 %all-to-all-start.3 = ((bf16[32,3,2048]{2,1,0:T(4,128)(2,1)}), bf16[32,3,2048]{2,1,0:T(4,128)(2,1)}, u32[]{:S(2)}, u32[]{:S(2)}) async-start(bf16[32,3,2048]{2,1,0:T(4,128)(2,1)} %all_to_all.55), calls=%async_computation.3 | async-start | bytes 1048576 | tf_op jit(solution)/shard_map/all_to_all | solution.py:56
  381.5 10.2 %conditional.7 = (bf16[2,192,2048]{2,1,0:T(8,128)(2,1)S(1)}) conditional(s32[]{:T(128)} %convert_element_type.189, () %tuple.44, (bf16[192,2048]{1,0:T(8,128)(2,1)}, bf16[384,2,2048]{2,1,0:T(2,128)(2,1)S(1)}, bf16[192,2048]{1,0:T(8,128)(2,1)}) %tuple.115), branch_computations={%region_27.29_spmd, %region_28.30_spmd} | conditional | flops 1213071360 | bytes 52789368 | solution.py:182
  384.9 4.8 fusion.25
  393.7 21.0 %all-to-all-done.3 = bf16[32,3,2048]{2,1,0:T(4,128)(2,1)} async-done(((bf16[32,3,2048]{2,1,0:T(4,128)(2,1)}), bf16[32,3,2048]{2,1,0:T(4,128)(2,1)}, u32[]{:S(2)}, u32[]{:S(2)}) %all-to-all-start.3) | async-done | bytes 393248 | tf_op jit(solution)/shard_map/all_to_all | solution.py:56
  418.6 3.9 all-to-all-start.4
  422.6 14.1 %collective-permute-done.1 = bf16[2,192,2048]{2,1,0:T(8,128)(2,1)} collective-permute-done((bf16[2,192,2048]{2,1,0:T(8,128)(2,1)S(1)}, bf16[2,192,2048]{2,1,0:T(8,128)(2,1)}, u32[]{:S(2)}, u32[]{:S(2)}) %collective-permute-start.1) | collective-permute-done | bytes 1572896 | tf_op jit(solution)/shard_map/ppermute | solution.py:11
  438.4 10.9 %all-to-all-done.4 = bf16[32,2,3072]{2,1,0:T(2,128)(2,1)S(1)} async-done(((bf16[32,2,3072]{2,1,0:T(2,128)(2,1)}), bf16[32,2,3072]{2,1,0:T(2,128)(2,1)S(1)}, u32[]{:S(2)}, u32[]{:S(2)}) %all-to-all-start.4) | async-done | bytes 393248 | tf_op jit(solution)/shard_map/all_to_all | solution.py:50
  450.4 26.3 %all-gather.13.cloned.1.call-done = bf16[768,2048]{1,0:T(8,128)(2,1)} async-done(((bf16[96,2048]{1,0:T(8,128)(2,1)}), bf16[768,2048]{1,0:T(8,128)(2,1)}) %all-gather.13.cloned.1.call-update) | async-done | bytes 3145744 | tf_op jit(solution)/shard_map/all_gather | solution.py:55
  480.2 13.2 %all-to-all-start.7 = ((bf16[32,3,2048]{2,1,0:T(4,128)(2,1)}), bf16[32,3,2048]{2,1,0:T(4,128)(2,1)S(1)}, u32[]{:S(2)}, u32[]{:S(2)}) async-start(bf16[32,3,2048]{2,1,0:T(4,128)(2,1)} %all_to_all.61), calls=%async_computation.7 | async-start | bytes 1048576 | tf_op jit(solution)/shard_map/all_to_all | solution.py:56
  493.5 33.3 %all-to-all-done.7 = bf16[32,3,2048]{2,1,0:T(4,128)(2,1)S(1)} async-done(((bf16[32,3,2048]{2,1,0:T(4,128)(2,1)}), bf16[32,3,2048]{2,1,0:T(4,128)(2,1)S(1)}, u32[]{:S(2)}, u32[]{:S(2)}) %all-to-all-start.7) | async-done | bytes 393248 | tf_op jit(solution)/shard_map/all_to_all | solution.py:56
  529.7 3.9 all-to-all-start.8
  533.7 27.0 %all-to-all-done.8 = bf16[32,2,3072]{2,1,0:T(2,128)(2,1)S(1)} async-done(((bf16[32,2,3072]{2,1,0:T(2,128)(2,1)}), bf16[32,2,3072]{2,1,0:T(2,128)(2,1)S(1)}, u32[]{:S(2)}, u32[]{:S(2)}) %all-to-all-start.8) | async-done | bytes 393248 | tf_op jit(solution)/shard_map/all_to_all | solution.py:50
  561.8 26.3 %all-gather.15.cloned.1.call-done = bf16[768,2048]{1,0:T(8,128)(2,1)} async-done(((bf16[96,2048]{1,0:T(8,128)(2,1)}), bf16[768,2048]{1,0:T(8,128)(2,1)}) %all-gather.15.cloned.1.call-update) | async-done | bytes 3145744 | tf_op jit(solution)/shard_map/all_gather | solution.py:55
  590.8 46.4 %all_to_all.78 = bf16[32,3,2048]{2,1,0:T(4,128)(2,1)S(1)} all-to-all(bf16[32,3,2048]{2,1,0:T(4,128)(2,1)S(1)} %all_to_all.65), channel_id=1, replica_groups=mesh['sect'=2,'exp'=32,'dp'=8] {'exp'}, dimensions={0} | all-to-all | bytes 786432 | tf_op jit(solution)/shard_map/all_to_all | solution.py:56
  637.8 2.7 collective-permute-start.2
  640.6 4.9 collective-permute-done.2
  (173 shorter events, 62.1 us)
Async XLA Ops:
  16.1 45.0 %copy-start.14 = (bf16[1,1,192,2048]{3,2,1,0:T(8,128)(2,1)S(1)}, bf16[1,1,192,2048]{3,2,1,0:T(8,128)(2,1)}, u32[]{:S(2)}) copy-start(bf16[1,1,192,2048]{3,2,1,0:T(8,128)(2,1)} %param.28) | copy-start | bytes 2359300
  17.1 43.7 %all-to-all-start = ((bf16[32,2,3072]{2,1,0:T(2,128)(2,1)}), bf16[32,2,3072]{2,1,0:T(2,128)(2,1)S(1)}, u32[]{:S(2)}, u32[]{:S(2)}) async-start(bf16[32,2,3072]{2,1,0:T(2,128)(2,1)} %reshape.301), calls=%async_computation | async-start | bytes 786432 | tf_op jit(solution)/shard_map/all_to_all | solution.py:50
  33.3 56.2 %all-gather.9.cloned.1.call-start = ((), (), s32[]{:S(2)}) async-start(), calls=%async_computation.10 | async-start | bytes 3538944 | tf_op jit(solution)/shard_map/all_gather | solution.py:55
  61.1 0.9 copy-start.9
  61.1 1.1 copy-start.10
  61.2 0.7 copy-start.2
  61.2 6.3 copy-start.13
  61.2 6.7 %copy-start.16 = (s32[1,32]{1,0:T(1,128)S(1)}, s32[1,32]{1,0:T(1,128)}, u32[]{:S(2)}) copy-start(s32[1,32]{1,0:T(1,128)} %param.33) | copy-start | bytes 388
  63.1 43.6 %collective-permute-start = (bf16[32,2,2048]{2,1,0:T(2,128)(2,1)S(1)}, bf16[32,2,2048]{2,1,0:T(2,128)(2,1)S(1)}, u32[]{:S(2)}, u32[]{:S(2)}) collective-permute-start(bf16[32,2,2048]{2,1,0:T(2,128)(2,1)S(1)} %pad_maximum_fusion.2), channel_id=1, source_target_pairs={{0,256},{256,0},{1,257},{257,1},{2,258},{258,2},{3,259},{259,3},{4... | collective-permute-start | bytes 786440 | tf_op jit(solution)/shard_map/ppermute | solution.py:11
  93.1 46.6 %all-to-all-start.1 = ((bf16[32,3,2048]{2,1,0:T(4,128)(2,1)}), bf16[32,3,2048]{2,1,0:T(4,128)(2,1)S(1)}, u32[]{:S(2)}, u32[]{:S(2)}) async-start(bf16[32,3,2048]{2,1,0:T(4,128)(2,1)} %all_to_all.51), calls=%async_computation.1 | async-start | bytes 1048576 | tf_op jit(solution)/shard_map/all_to_all | solution.py:56
  112.7 31.1 %copy-start.11 = (s32[128,2]{0,1:T(2,128)S(1)}, s32[128,2]{0,1:T(2,128)}, u32[]{:S(2)}) copy-start(s32[128,2]{0,1:T(2,128)} %param.34) | copy-start | bytes 3076
  112.7 32.8 %copy-start.6 = (bf16[32,2048]{1,0:T(8,128)(2,1)S(1)}, bf16[32,2048]{1,0:T(8,128)(2,1)}, u32[]{:S(2)}) copy-start(bf16[32,2048]{1,0:T(8,128)(2,1)} %param.24) | copy-start | bytes 393220
  139.7 57.4 %all-to-all-start.5 = ((bf16[128,2,2048]{2,1,0:T(2,128)(2,1)}), bf16[128,2,2048]{2,1,0:T(2,128)(2,1)S(1)}, u32[]{:S(2)}, u32[]{:S(2)}) async-start(bf16[128,2,2048]{2,1,0:T(2,128)(2,1)} %broadcast_select_fusion.1), calls=%async_computation.5 | async-start | bytes 2097152 | tf_op jit(solution)/shard_map/all_to_all | solution.py:170
  143.8 2.1 copy-start.8
  197.1 32.2 %all-to-all-start.2 = ((bf16[32,2,3072]{2,1,0:T(2,128)(2,1)}), bf16[32,2,3072]{2,1,0:T(2,128)(2,1)S(1)}, u32[]{:S(2)}, u32[]{:S(2)}) async-start(bf16[32,2,3072]{2,1,0:T(2,128)(2,1)} %reshape.303), calls=%async_computation.2 | async-start | bytes 786432 | tf_op jit(solution)/shard_map/all_to_all | solution.py:50
  229.2 0.7 copy-start.5
  230.0 143.1 %all-to-all-start.6 = ((bf16[384,2,2048]{2,1,0:T(2,128)(2,1)}), bf16[384,2,2048]{2,1,0:T(2,128)(2,1)S(1)}, u32[]{:S(2)}, u32[]{:S(2)}) async-start(bf16[384,2,2048]{2,1,0:T(2,128)(2,1)} %copy.159), calls=%async_computation.6 | async-start | bytes 6291456 | tf_op jit(solution)/shard_map/all_to_all | solution.py:50
  234.1 40.7 %all-gather.11.cloned.1.call-start = ((), (), s32[]{:S(2)}) async-start(), calls=%async_computation.11 | async-start | bytes 3538944 | tf_op jit(solution)/shard_map/all_gather | solution.py:55
  373.1 41.6 %all-to-all-start.3 = ((bf16[32,3,2048]{2,1,0:T(4,128)(2,1)}), bf16[32,3,2048]{2,1,0:T(4,128)(2,1)}, u32[]{:S(2)}, u32[]{:S(2)}) async-start(bf16[32,3,2048]{2,1,0:T(4,128)(2,1)} %all_to_all.55), calls=%async_computation.3 | async-start | bytes 1048576 | tf_op jit(solution)/shard_map/all_to_all | solution.py:56
  381.8 1.4 copy-start.15
  383.1 1.7 copy-start
  384.9 4.8 copy-start.1
  389.6 1.9 copy-start.7
  391.7 44.9 %collective-permute-start.1 = (bf16[2,192,2048]{2,1,0:T(8,128)(2,1)S(1)}, bf16[2,192,2048]{2,1,0:T(8,128)(2,1)}, u32[]{:S(2)}, u32[]{:S(2)}) collective-permute-start(bf16[2,192,2048]{2,1,0:T(8,128)(2,1)S(1)} %get-tuple-element.162), channel_id=1, source_target_pairs={{0,256},{256,0},{1,257},{257,1},{2,258},{258,2},{3,259},{259,3},{4... | collective-permute-start | bytes 4718600 | tf_op jit(solution)/shard_map/ppermute | solution.py:11
  418.6 30.6 %all-to-all-start.4 = ((bf16[32,2,3072]{2,1,0:T(2,128)(2,1)}), bf16[32,2,3072]{2,1,0:T(2,128)(2,1)S(1)}, u32[]{:S(2)}, u32[]{:S(2)}) async-start(bf16[32,2,3072]{2,1,0:T(2,128)(2,1)} %reshape.305), calls=%async_computation.4 | async-start | bytes 786432 | tf_op jit(solution)/shard_map/all_to_all | solution.py:50
  422.5 54.2 %all-gather.13.cloned.1.call-start = ((), (), s32[]{:S(2)}) async-start(), calls=%async_computation.12 | async-start | bytes 3538944 | tf_op jit(solution)/shard_map/all_gather | solution.py:55
  449.7 0.7 copy-start.3
  480.2 46.6 %all-to-all-start.7 = ((bf16[32,3,2048]{2,1,0:T(4,128)(2,1)}), bf16[32,3,2048]{2,1,0:T(4,128)(2,1)S(1)}, u32[]{:S(2)}, u32[]{:S(2)}) async-start(bf16[32,3,2048]{2,1,0:T(4,128)(2,1)} %all_to_all.61), calls=%async_computation.7 | async-start | bytes 1048576 | tf_op jit(solution)/shard_map/all_to_all | solution.py:56
  529.7 30.9 %all-to-all-start.8 = ((bf16[32,2,3072]{2,1,0:T(2,128)(2,1)}), bf16[32,2,3072]{2,1,0:T(2,128)(2,1)S(1)}, u32[]{:S(2)}, u32[]{:S(2)}) async-start(bf16[32,2,3072]{2,1,0:T(2,128)(2,1)} %reshape.307), calls=%async_computation.8 | async-start | bytes 786432 | tf_op jit(solution)/shard_map/all_to_all | solution.py:50
  533.6 54.5 %all-gather.15.cloned.1.call-start = ((), (), s32[]{:S(2)}) async-start(), calls=%async_computation.13 | async-start | bytes 3538944 | tf_op jit(solution)/shard_map/all_gather | solution.py:55
  561.0 0.7 copy-start.4
  637.8 7.7 %collective-permute-start.2 = (bf16[32,1024]{1,0:T(8,128)(2,1)S(1)}, bf16[32,1024]{1,0:T(8,128)(2,1)S(1)}, u32[]{:S(2)}, u32[]{:S(2)}) collective-permute-start(bf16[32,1024]{1,0:T(8,128)(2,1)S(1)} %slice.87), channel_id=1, source_target_pairs={{0,256},{256,0},{1,257},{257,1},{2,258},{258,2},{3,259},{259,3},{4... | collective-permute-start | bytes 196616 | tf_op jit(solution)/shard_map/ppermute | solution.py:11
  (1 other events, 0.7 us)
Sparse Core Ops, SparseCore 0:
  62.1 27.3 all-gather.8
  238.5 36.1 all-gather.10
  450.6 26.1 all-gather.12
  561.9 26.1 all-gather.14
